TPU v7x, 32 devices: a whole 2x2x4 slice. The times are simulated.
32 devices in a mesh: row: 4 (over y, x), col: 8 (over z, core).
Axes of the slice: x: 2, y: 2, z: 4, core: 2. Of those that a mesh axis runs over, the one named last changes fastest.
Arguments:
- trail: bfloat16 [1024, 24576], P('row', 'col'), may hold values from -6 to 6
- trail_rows: int32 [16, 192], P('row', 'col'), may hold values from 0 to 47, as said below
- owner_x: bfloat16 [16384, 1024], P(('row', 'col')), may hold values from -0.1875 to 0.1875
- owner_y: bfloat16 [16384, 1024], P(('row', 'col')), may hold values from -6 to 6
- owner_of: int32 [192], replicated, may hold values from 0 to 7, as said below
- inv_first: bfloat16 [2, 256, 256], replicated, may hold values from -0.25 to 0.25
- inv_second: bfloat16 [2, 256, 256], replicated, may hold values from -0.25 to 0.25
- couple_right: bfloat16 [2, 256, 256], replicated, may hold values from -0.25 to 0.25
- couple_left: bfloat16 [2, 256, 256], replicated, may hold values from -0.25 to 0.25
Outputs:
- updated_trail: bfloat16 [1024, 24576], P('row', 'col')
Inputs may be any that keep to these rules, and one draw needn't show every extreme that they name: `trail_rows`: for each grid row and each block column, the 4 entries in rows r * 4 to r * 4 + 3 are distinct local block rows. `owner_of`: the 6 blocks r * 48 + c * 6 + k (k < 6) have distinct owners; one owner holds at most 8 blocks of its grid row, and some owner of every grid row holds exactly 8.
All inputs are finite; a program needn't handle non-finite values.
Results may differ from a plain program's by a relative error of at most 0.0062.
Values may be sent and summed in bfloat16 or wider, within the bound.
A program may use at most 128 MiB of HBM per device.

v0:
```python
import jax
import jax.numpy as jnp
from jax import lax
from jax.sharding import PartitionSpec as P

BS = 64
PANEL = 256
PER = 6


def real_form(pair):
    top_rows = jnp.concatenate([pair[0], pair[1]], axis=1)
    low_rows = jnp.concatenate([-pair[1], pair[0]], axis=1)
    return jnp.concatenate([top_rows, low_rows], axis=0)


def halves(matrix):
    first_half = jnp.concatenate([matrix[:, :PANEL], matrix[:, 2 * PANEL : 3 * PANEL]], axis=1)
    second_half = jnp.concatenate([matrix[:, PANEL : 2 * PANEL], matrix[:, 3 * PANEL :]], axis=1)
    return (first_half, second_half)


def join_panels(left_part, right_part):
    return jnp.concatenate(
        [left_part[:, :PANEL], right_part[:, :PANEL], left_part[:, PANEL:], right_part[:, PANEL:]],
        axis=1,
    )


def form_rows(matrix, inv_first, inv_second, couple_right):
    first_half, second_half = halves(matrix)
    low_first = jnp.dot(
        first_half, real_form(inv_first), preferred_element_type=jnp.float32
    ).astype(jnp.bfloat16)
    remainder = second_half.astype(jnp.float32) - jnp.dot(
        low_first, real_form(couple_right), preferred_element_type=jnp.float32
    )
    remainder = remainder.astype(jnp.bfloat16)
    low_second = jnp.dot(
        remainder, real_form(inv_second), preferred_element_type=jnp.float32
    ).astype(jnp.bfloat16)
    return join_panels(low_first, low_second)


def form_cols(matrix, inv_first, couple_left):
    coupling = jnp.dot(
        jnp.concatenate([couple_left[0], couple_left[1]], axis=1),
        real_form(inv_first),
        preferred_element_type=jnp.float32,
    ).astype(jnp.bfloat16)
    transposed = jnp.stack([coupling[:, :PANEL].T, coupling[:, PANEL:].T])
    first_half, second_half = halves(matrix)
    remainder = second_half.astype(jnp.float32) - jnp.dot(
        first_half, real_form(transposed), preferred_element_type=jnp.float32
    )
    return join_panels(first_half, remainder.astype(jnp.bfloat16))


def stack_cols(upper_rows):
    count = upper_rows.shape[0] // BS
    real_part = upper_rows[:, : 2 * PANEL]
    imag_part = upper_rows[:, 2 * PANEL :]
    top_rows = jnp.concatenate([real_part, -imag_part], axis=1).reshape(count, BS, 4 * PANEL)
    low_rows = jnp.concatenate([imag_part, real_part], axis=1).reshape(count, BS, 4 * PANEL)
    return jnp.concatenate([top_rows, low_rows], axis=1)


def local(
    trail, trail_rows, owner_x, owner_y, owner_of, inv_first, inv_second, couple_right, couple_left
):
    col_count = lax.axis_size("col")
    my_row = lax.axis_index("row")
    my_col = lax.axis_index("col")
    row_width = 4 * PANEL
    row_blocks = PER * col_count
    owners = lax.dynamic_slice_in_dim(owner_of, my_row * row_blocks, row_blocks)
    owner_marks = (owners[:, None] == jnp.arange(col_count, dtype=jnp.int32)[None, :]).astype(
        jnp.int32
    )
    before = jnp.cumsum(owner_marks, axis=0, dtype=jnp.int32) - owner_marks
    slot_index = jnp.sum(before * owner_marks, axis=1, dtype=jnp.int32).reshape(col_count, PER)
    owner_grid = owners.reshape(col_count, PER)
    my_marks = (owner_grid == my_col).astype(jnp.int32)
    send_slots = jnp.sum(my_marks * slot_index, axis=1, dtype=jnp.int32)
    held_x = owner_x.reshape(-1, BS, row_width)
    held_y = owner_y.reshape(-1, BS, row_width)
    got_x, got_y = (
        lax.all_to_all(held_x[send_slots], "col", split_axis=0, concat_axis=0, tiled=True),
        lax.all_to_all(held_y[send_slots], "col", split_axis=0, concat_axis=0, tiled=True),
    )
    sources = lax.dynamic_index_in_dim(owner_grid, my_col, 0, keepdims=False)
    own_x = got_x[sources].reshape(PER * BS, row_width)
    own_y = got_y[sources].reshape(PER * BS, row_width)
    lower_rows = form_rows(
        lax.all_gather(own_x, "col", axis=0, tiled=True), inv_first, inv_second, couple_right
    )
    upper_rows = form_cols(lax.all_gather(own_y, "row", axis=0, tiled=True), inv_first, couple_left)
    stacked = stack_cols(upper_rows)
    column_count = stacked.shape[0]
    lower_blocks = lower_rows.reshape(-1, BS, row_width)
    trail_tiles = trail.reshape(-1, BS, column_count, 2 * BS)

    def one_slot(inputs):
        block_tile, pattern_rows = inputs
        picked = lower_blocks[pattern_rows]
        change = jnp.einsum("jbp,jqp->bjq", picked, stacked, preferred_element_type=jnp.float32)
        return (block_tile.astype(jnp.float32) - change).astype(jnp.bfloat16)

    updated = lax.map(one_slot, (trail_tiles, trail_rows))
    return updated.reshape(trail.shape)


def solution(mesh):
    placed = (
        P("row", "col"),
        P("row", "col"),
        P(("row", "col"), None),
        P(("row", "col"), None),
        P(),
        P(),
        P(),
        P(),
        P(),
    )
    return jax.shard_map(
        local, mesh=mesh, in_specs=placed, out_specs=P("row", "col"), check_vma=False
    )
```

profile of v0, /device:TPU:0, one launch (start us, length us, event | category | flops | bytes accessed | tf_op | source)
XLA Modules:
  0.0 239.3 jit_solution(10763192760506426968)
XLA Ops:
  8.0 1.6 gather_fusion.3
  9.6 6.3 %all-to-all-start.1 = ((bf16[8,64,1024]{2,1,0:T(8,128)(2,1)}), bf16[8,64,1024]{2,1,0:T(8,128)(2,1)S(1)}, u32[]{:S(2)}, u32[]{:S(2)}) async-start(bf16[8,64,1024]{2,1,0:T(8,128)(2,1)} %gather_fusion.3), calls=%async_computation.1 | async-start | bytes 2097152 | tf_op jit(solution)/shard_map/all_to_all | solution.py:89
  16.0 26.5 %all-to-all-done.1 = bf16[8,64,1024]{2,1,0:T(8,128)(2,1)S(1)} async-done(((bf16[8,64,1024]{2,1,0:T(8,128)(2,1)}), bf16[8,64,1024]{2,1,0:T(8,128)(2,1)S(1)}, u32[]{:S(2)}, u32[]{:S(2)}) %all-to-all-start.1) | async-done | bytes 1048608 | tf_op jit(solution)/shard_map/all_to_all | solution.py:89
  42.5 1.5 gather_fusion.4
  44.8 29.0 %all_to_all.10 = bf16[8,64,1024]{2,1,0:T(8,128)(2,1)S(1)} all-to-all(bf16[8,64,1024]{2,1,0:T(8,128)(2,1)S(1)} %gather_fusion.1), channel_id=1, replica_groups=mesh['row'=4,'col'=8] {'col'}, dimensions={0} | all-to-all | bytes 2097152 | tf_op jit(solution)/shard_map/all_to_all | solution.py:88
  73.8 1.6 gather_fusion.2
  75.4 2.9 %copy.18 = bf16[32,8,24,128]{3,2,1,0:T(8,128)(2,1)} copy(bf16[32,8,24,128]{3,1,2,0:T(8,128)(2,1)} %bitcast.102) | data formatting | bytes 3145728
  79.6 7.5 %all-gather.5.cloned.1.call-done = bf16[1536,1024]{1,0:T(8,128)(2,1)} async-done(((bf16[384,1024]{1,0:T(8,128)(2,1)}), bf16[1536,1024]{1,0:T(8,128)(2,1)}) %all-gather.5.cloned.1.call-update) | async-done | bytes 3145744 | tf_op jit(solution)/shard_map/all_gather | solution.py:97
  87.1 2.1 fusion.54
  91.3 3.1 %pad_maximum_fusion.1 = bf16[24,128,1024]{2,1,0:T(8,128)(2,1)} fusion(bf16[24,64,1024]{2,1,0:T(8,128)(2,1)S(1)} %bitcast.95, bf16[24,64,512]{2,1,0:T(8,128)(2,1)S(1)} %maximum_negate_fusion, bf16[24,64,512]{2,1,0:T(8,128)(2,1)S(1)} %bitcast.99), kind=kLoop, calls=%fused_computation.18 | loop fusion | flops 18874368 | bytes 12582912 | tf_op jit(solution)/shard_map/concatenate | solution.py:65
  94.4 59.1 %all-gather.3.cloned.1.call-done = bf16[3072,1024]{1,0:T(8,128)(2,1)} async-done(((bf16[384,1024]{1,0:T(8,128)(2,1)}), bf16[3072,1024]{1,0:T(8,128)(2,1)}) %all-gather.3.cloned.1.call-update) | async-done | bytes 6291472 | tf_op jit(solution)/shard_map/all_gather | solution.py:95
  153.6 4.9 %fusion.53 = (bf16[3072,256]{1,0:T(8,128)(2,1)}, bf16[3072,256]{1,0:T(8,128)(2,1)}, bf16[3072,256]{1,0:T(8,128)(2,1)S(1)}, bf16[3072,256]{1,0:T(8,128)(2,1)S(1)}) fusion(bf16[3072,1024]{1,0:T(8,128)(2,1)} %all-gather.3.cloned.1.call-done), kind=kLoop, calls=%fused_computation.87 | loop fusion | bytes 12582912 | tf_op jit(solution)/shard_map/slice | solution.py:19
  158.5 1.9 convolution_convert_fusion.1
  160.6 1.5 copy-done.2
  162.1 8.1 %convolution_convert_fusion = bf16[3072,512]{0,1:T(8,128)(2,1)} fusion(bf16[3072,512]{0,1:T(8,128)(2,1)} %copy-done.2, bf16[3072,256]{1,0:T(8,128)(2,1)} %get-tuple-element.63, bf16[3072,256]{1,0:T(8,128)(2,1)} %get-tuple-element.62, bf16[256,256]{1,0:T(8,128)(2,1)} %get-tuple-element.86, bf16[256,256]{1,0:T(8,128)(2,1)S(1)} %get-tuple-element.88, ...), kind=kOutput, calls=%fused_computation.20 | convolution fusion | flops 3236429824 | bytes 10223616 | tf_op jit(solution)/shard_map/dot_general | solution.py:39
  170.2 2.1 fusion.56
  172.3 3.2 %pad_maximum_fusion = bf16[3072,1024]{0,1:T(8,128)(2,1)} fusion(bf16[3072,256]{0,1:T(8,128)(2,1)S(1)} %get-tuple-element.73, bf16[3072,256]{0,1:T(8,128)(2,1)S(1)} %get-tuple-element.71, bf16[3072,256]{0,1:T(8,128)(2,1)S(1)} %get-tuple-element.72, bf16[3072,256]{0,1:T(8,128)(2,1)S(1)} %get-tuple-element.70), kind=kLoop, calls=%fused_computation.17 | loop fusion | flops 25165824 | bytes 12582912 | tf_op jit(solution)/shard_map/concatenate | solution.py:24
  175.5 8.6 %copy.12 = bf16[3072,1024]{1,0:T(8,128)(2,1)} copy(bf16[3072,1024]{0,1:T(8,128)(2,1)} %pad_maximum_fusion) | data formatting | bytes 12582912 | tf_op jit(solution)/shard_map/concatenate | solution.py:24
  184.1 45.4 %while.10 = (s32[]{:T(128)}, bf16[4,64,24,128]{3,2,1,0:T(8,128)(2,1)}, bf16[4,64,24,128]{3,2,1,0:T(8,128)(2,1)}, s32[4,24]{1,0:T(4,128)}, bf16[48,64,1024]{2,1,0...) while((s32[]{:T(128)}, bf16[4,64,24,128]{3,2,1,0:T(8,128)(2,1)}, ...), condition=%wide.region_4.5_spmd, body=%wide.region_3.4_spmd.sunk | while | flops 403244096 | bytes 18093012 | solution.py:109
  184.8 3.5 %gather_fusion = bf16[24,64,1024]{2,1,0:T(8,128)(2,1)S(1)} fusion(bf16[48,64,1024]{2,1,0:T(8,128)(2,1)} %get-tuple-element.145, s32[1024]{0:T(1024)S(1)} %pad_clamp_fusion.4), kind=kCustom, calls=%fused_computation.clone.1 | custom fusion | bytes 6291552 | tf_op jit(solution)/shard_map/while/body/eval_jaxpr/gather | solution.py:105
  188.4 1.0 constant_dynamic-slice_fusion.3
  189.4 5.1 %fusion.68 = bf16[1,64,24,128]{3,1,2,0:T(8,128)(2,1)S(1)} fusion(bf16[24,64,1024]{2,1,0:T(8,128)(2,1)S(1)} %gather_fusion, bf16[24,128,1024]{2,1,0:T(8,128)(2,1)} %get-tuple-element.146, bf16[1,64,24,128]{3,2,1,0:T(8,128)(2,1)S(1)} %constant_dynamic-slice_fusion.3), kind=kOutput, calls=%fused_computation.8.clone.1 | convolution fusion | flops 403243008 | bytes 10223616 | tf_op jit(solution)/shard_map/while/body/eval_jaxpr/jbp,jqp->bjq/dot_general | solution.py:106
  196.2 3.5 %gather_fusion = bf16[24,64,1024]{2,1,0:T(8,128)(2,1)S(1)} fusion(bf16[48,64,1024]{2,1,0:T(8,128)(2,1)} %get-tuple-element.145, s32[1024]{0:T(1024)S(1)} %pad_clamp_fusion.4), kind=kCustom, calls=%fused_computation.clone.1 | custom fusion | bytes 6291552 | tf_op jit(solution)/shard_map/while/body/eval_jaxpr/gather | solution.py:105
  199.7 1.0 constant_dynamic-slice_fusion.3
  200.8 5.1 %fusion.68 = bf16[1,64,24,128]{3,1,2,0:T(8,128)(2,1)S(1)} fusion(bf16[24,64,1024]{2,1,0:T(8,128)(2,1)S(1)} %gather_fusion, bf16[24,128,1024]{2,1,0:T(8,128)(2,1)} %get-tuple-element.146, bf16[1,64,24,128]{3,2,1,0:T(8,128)(2,1)S(1)} %constant_dynamic-slice_fusion.3), kind=kOutput, calls=%fused_computation.8.clone.1 | convolution fusion | flops 403243008 | bytes 10223616 | tf_op jit(solution)/shard_map/while/body/eval_jaxpr/jbp,jqp->bjq/dot_general | solution.py:106
  207.5 3.5 %gather_fusion = bf16[24,64,1024]{2,1,0:T(8,128)(2,1)S(1)} fusion(bf16[48,64,1024]{2,1,0:T(8,128)(2,1)} %get-tuple-element.145, s32[1024]{0:T(1024)S(1)} %pad_clamp_fusion.4), kind=kCustom, calls=%fused_computation.clone.1 | custom fusion | bytes 6291552 | tf_op jit(solution)/shard_map/while/body/eval_jaxpr/gather | solution.py:105
  211.1 1.0 constant_dynamic-slice_fusion.3
  212.1 5.1 %fusion.68 = bf16[1,64,24,128]{3,1,2,0:T(8,128)(2,1)S(1)} fusion(bf16[24,64,1024]{2,1,0:T(8,128)(2,1)S(1)} %gather_fusion, bf16[24,128,1024]{2,1,0:T(8,128)(2,1)} %get-tuple-element.146, bf16[1,64,24,128]{3,2,1,0:T(8,128)(2,1)S(1)} %constant_dynamic-slice_fusion.3), kind=kOutput, calls=%fused_computation.8.clone.1 | convolution fusion | flops 403243008 | bytes 10223616 | tf_op jit(solution)/shard_map/while/body/eval_jaxpr/jbp,jqp->bjq/dot_general | solution.py:106
  218.9 3.5 %gather_fusion = bf16[24,64,1024]{2,1,0:T(8,128)(2,1)S(1)} fusion(bf16[48,64,1024]{2,1,0:T(8,128)(2,1)} %get-tuple-element.145, s32[1024]{0:T(1024)S(1)} %pad_clamp_fusion.4), kind=kCustom, calls=%fused_computation.clone.1 | custom fusion | bytes 6291552 | tf_op jit(solution)/shard_map/while/body/eval_jaxpr/gather | solution.py:105
  222.4 1.0 constant_dynamic-slice_fusion.3
  223.5 5.1 %fusion.68 = bf16[1,64,24,128]{3,1,2,0:T(8,128)(2,1)S(1)} fusion(bf16[24,64,1024]{2,1,0:T(8,128)(2,1)S(1)} %gather_fusion, bf16[24,128,1024]{2,1,0:T(8,128)(2,1)} %get-tuple-element.146, bf16[1,64,24,128]{3,2,1,0:T(8,128)(2,1)S(1)} %constant_dynamic-slice_fusion.3), kind=kOutput, calls=%fused_computation.8.clone.1 | convolution fusion | flops 403243008 | bytes 10223616 | tf_op jit(solution)/shard_map/while/body/eval_jaxpr/jbp,jqp->bjq/dot_general | solution.py:106
  229.6 3.0 %copy.25 = bf16[32,8,24,128]{3,1,2,0:T(8,128)(2,1)} copy(bf16[32,8,24,128]{3,2,1,0:T(8,128)(2,1)} %bitcast.33) | data formatting | bytes 3145728
  (58 shorter events, 12.5 us)
Async XLA Ops:
  6.5 1.5 copy-start
  8.0 36.1 %copy-start.3 = (bf16[512,1024]{1,0:T(8,128)(2,1)S(1)}, bf16[512,1024]{1,0:T(8,128)(2,1)}, u32[]{:S(2)}) copy-start(bf16[512,1024]{1,0:T(8,128)(2,1)} %param.13) | copy-start | bytes 3145732
  9.6 32.9 %all-to-all-start.1 = ((bf16[8,64,1024]{2,1,0:T(8,128)(2,1)}), bf16[8,64,1024]{2,1,0:T(8,128)(2,1)S(1)}, u32[]{:S(2)}, u32[]{:S(2)}) async-start(bf16[8,64,1024]{2,1,0:T(8,128)(2,1)} %gather_fusion.3), calls=%async_computation.1 | async-start | bytes 2097152 | tf_op jit(solution)/shard_map/all_to_all | solution.py:89
  16.0 71.2 %all-gather.5.cloned.1.call-start = ((), (), s32[]{:S(2)}) async-start(), calls=%async_computation.3 | async-start | bytes 3932160 | tf_op jit(solution)/shard_map/all_gather | solution.py:97
  44.1 109.5 %all-gather.3.cloned.1.call-start = ((), (), s32[]{:S(2)}) async-start(), calls=%async_computation.2 | async-start | bytes 7077888 | tf_op jit(solution)/shard_map/all_gather | solution.py:95
  73.8 4.6 %copy-start.4 = (bf16[2,256,256]{2,1,0:T(8,128)(2,1)S(1)}, bf16[2,256,256]{2,1,0:T(8,128)(2,1)}, u32[]{:S(2)}) copy-start(bf16[2,256,256]{2,1,0:T(8,128)(2,1)} %param.16) | copy-start | bytes 786436
  73.8 4.6 %copy-start.7 = (bf16[2,256,256]{2,1,0:T(8,128)(2,1)S(1)}, bf16[2,256,256]{2,1,0:T(8,128)(2,1)}, u32[]{:S(2)}) copy-start(bf16[2,256,256]{2,1,0:T(8,128)(2,1)} %param.19) | copy-start | bytes 786436
  75.4 3.4 %copy-start.5 = (bf16[2,256,256]{2,1,0:T(8,128)(2,1)S(1)}, bf16[2,256,256]{2,1,0:T(8,128)(2,1)}, u32[]{:S(2)}) copy-start(bf16[2,256,256]{2,1,0:T(8,128)(2,1)} %param.17) | copy-start | bytes 786436
  75.4 3.4 %copy-start.6 = (bf16[2,256,256]{2,1,0:T(8,128)(2,1)S(1)}, bf16[2,256,256]{2,1,0:T(8,128)(2,1)}, u32[]{:S(2)}) copy-start(bf16[2,256,256]{2,1,0:T(8,128)(2,1)} %param.18) | copy-start | bytes 786436
  160.4 1.7 copy-start.2
  229.5 3.0 %copy-start.1 = (bf16[512,1024]{1,0:T(8,128)(2,1)S(1)}, bf16[512,1024]{1,0:T(8,128)(2,1)}, u32[]{:S(2)}) copy-start(bf16[512,1024]{1,0:T(8,128)(2,1)} %param.14) | copy-start | bytes 3145732
Sparse Core Ops, SparseCore 0:
  44.2 42.8 all-gather.4
  88.8 64.7 all-gather.2
where the time goes:
time: 240 us; the launch traced here: 239 us
  waiting for transfers between devices  93.2 us (39%)
  local copies, waits for them, and re-layouts  54.9 us (23%)
  matrix products  31.5 us (13%)
  blocking collectives  29 us (12%)
  between operations  13.7 us (6%)
  other arithmetic  10.6 us (4%)
  starting transfers between devices  6.4 us (3%)
    all_gather x1, waiting for transfers between devices, local(): lax.all_gather(own_x, 'col', axis=0, tiled=True)  59.1 us
    all_to_all x1, blocking collectives, local(): lax.all_to_all(held_x[send_slots], 'col', split_axis=0, concat_axis=0, ti...  29 us
    all_to_all x1, waiting for transfers between devices, local(): lax.all_to_all(held_y[send_slots], 'col', split_axis=0, concat_axis=0, ti...  26.5 us
    dot_general x4, matrix products, one_slot(): jnp.einsum('jbp,jqp->bjq', picked, stacked, preferred_element_type=jnp.fl...  20.2 us
    gather x4, local copies, waits for them, and re-layouts, one_slot(): picked = lower_blocks[pattern_rows]  14.1 us
    concatenate x1, local copies, waits for them, and re-layouts, join_panels(): jnp.concatenate([left_part[:, :PANEL], right_part[:, :PANEL], left_part[:...  8.62 us
    dot_general x1, matrix products, form_rows(): jnp.dot(remainder, real_form(inv_second), preferred_element_type=jnp.floa...  8.11 us
    all_gather x1, waiting for transfers between devices, local(): lax.all_gather(own_y, 'row', axis=0, tiled=True)  7.5 us
  transfers between devices with their start and end apart: 3, of which 3 were waited for; matrix products, arithmetic and copies ran while one was open for 6% of the time, Pallas kernels for 0%

commit v1 on v0

--- a/solution.py
+++ b/solution.py
@@ -6,6 +6,24 @@
 BS = 64
 PANEL = 256
 PER = 6
+
+
+def collect(shard, axis, dim):
+    ways, here, step = (lax.axis_size(axis), lax.axis_index(axis), shard.shape[dim])
+    lengths = [n * ways if d == dim else n for d, n in enumerate(shard.shape)]
+    full = lax.dynamic_update_slice_in_dim(
+        jnp.zeros(lengths, shard.dtype), shard, here * step, axis=dim
+    )
+    going_up = going_down = shard
+    for far in range(1, ways // 2 + 1):
+        going_up = lax.ppermute(going_up, axis, [(d, (d + 1) % ways) for d in range(ways)])
+        full = lax.dynamic_update_slice_in_dim(full, going_up, (here - far) % ways * step, axis=dim)
+        if 2 * far < ways:
+            going_down = lax.ppermute(going_down, axis, [(d, (d - 1) % ways) for d in range(ways)])
+            full = lax.dynamic_update_slice_in_dim(
+                full, going_down, (here + far) % ways * step, axis=dim
+            )
+    return full
 
 
 def real_form(pair):
@@ -91,9 +109,7 @@
     sources = lax.dynamic_index_in_dim(owner_grid, my_col, 0, keepdims=False)
     own_x = got_x[sources].reshape(PER * BS, row_width)
     own_y = got_y[sources].reshape(PER * BS, row_width)
-    lower_rows = form_rows(
-        lax.all_gather(own_x, "col", axis=0, tiled=True), inv_first, inv_second, couple_right
-    )
+    lower_rows = form_rows(collect(own_x, "col", 0), inv_first, inv_second, couple_right)
     upper_rows = form_cols(lax.all_gather(own_y, "row", axis=0, tiled=True), inv_first, couple_left)
     stacked = stack_cols(upper_rows)
     column_count = stacked.shape[0]

time: 240 us -> 221 us (0.921)
  the two profiles are of different devices: /device:TPU:0 before, /device:TPU:11 now
where the time goes in v1:
time: 221 us; the launch traced here: 219 us
  waiting for transfers between devices  81.9 us (37%)
  local copies, waits for them, and re-layouts  58.6 us (27%)
  matrix products  30.8 us (14%)
  starting transfers between devices  20 us (9%)
  other arithmetic  14 us (6%)
  between operations  13.7 us (6%)
    ppermute x3, waiting for transfers between devices, collect(): lax.ppermute(going_down, axis, [(d, (d - 1) % ways) for d in range(ways)])  58.9 us
    all_to_all x1, waiting for transfers between devices, local(): lax.all_to_all(held_x[send_slots], 'col', split_axis=0, concat_axis=0, ti...  23 us
    dot_general x4, matrix products, one_slot(): jnp.einsum('jbp,jqp->bjq', picked, stacked, preferred_element_type=jnp.fl...  20.2 us
    gather x4, local copies, waits for them, and re-layouts, one_slot(): picked = lower_blocks[pattern_rows]  14.1 us
    concatenate x1, local copies, waits for them, and re-layouts, join_panels(): jnp.concatenate([left_part[:, :PANEL], right_part[:, :PANEL], left_part[:...  8.63 us
    dot_general x1, matrix products, form_rows(): jnp.dot(remainder, real_form(inv_second), preferred_element_type=jnp.floa...  7.39 us
    ppermute x4, starting transfers between devices, collect(): lax.ppermute(going_up, axis, [(d, (d + 1) % ways) for d in range(ways)])  7.19 us
    all_to_all x1, starting transfers between devices, local(): lax.all_to_all(held_y[send_slots], 'col', split_axis=0, concat_axis=0, ti...  6.79 us
  transfers between devices with their start and end apart: 10, of which 4 were waited for; matrix products, arithmetic and copies ran while one was open for 19% of the time, Pallas kernels for 0%

profile of v1, /device:TPU:11, one launch (start us, length us, event | category | flops | bytes accessed | tf_op | source)
XLA Modules:
  0.0 219.2 jit_solution(12466023344631983052)
XLA Ops:
  8.1 1.6 gather_fusion.1
  9.7 5.6 %all-to-all-start = ((bf16[8,64,1024]{2,1,0:T(8,128)(2,1)}), bf16[8,64,1024]{2,1,0:T(8,128)(2,1)S(1)}, u32[]{:S(2)}, u32[]{:S(2)}) async-start(bf16[8,64,1024]{2,1,0:T(8,128)(2,1)} %gather_fusion.1), calls=%async_computation | async-start | bytes 2097152 | tf_op jit(solution)/shard_map/all_to_all | solution.py:106
  15.3 23.0 %all-to-all-done = bf16[8,64,1024]{2,1,0:T(8,128)(2,1)S(1)} async-done(((bf16[8,64,1024]{2,1,0:T(8,128)(2,1)}), bf16[8,64,1024]{2,1,0:T(8,128)(2,1)S(1)}, u32[]{:S(2)}, u32[]{:S(2)}) %all-to-all-start) | async-done | bytes 1048608 | tf_op jit(solution)/shard_map/all_to_all | solution.py:106
  39.0 1.8 collective-permute-start
  40.7 1.6 gather_fusion.3
  42.4 6.8 %all-to-all-start.1 = ((bf16[8,64,1024]{2,1,0:T(8,128)(2,1)}), bf16[8,64,1024]{2,1,0:T(8,128)(2,1)S(1)}, u32[]{:S(2)}, u32[]{:S(2)}) async-start(bf16[8,64,1024]{2,1,0:T(8,128)(2,1)} %gather_fusion.3), calls=%async_computation.1 | async-start | bytes 2097152 | tf_op jit(solution)/shard_map/all_to_all | solution.py:107
  50.5 1.7 collective-permute-start.2
  54.5 39.0 %collective-permute-done.1 = bf16[384,1024]{1,0:T(8,128)(2,1)} collective-permute-done((bf16[384,1024]{1,0:T(8,128)(2,1)S(1)}, bf16[384,1024]{1,0:T(8,128)(2,1)}, u32[]{:S(2)}, u32[]{:S(2)}) %collective-permute-start.1) | collective-permute-done | bytes 786464 | tf_op jit(solution)/shard_map/ppermute | solution.py:22
  95.7 1.7 collective-permute-start.4
  98.3 1.7 fusion.58
  100.0 1.9 slice_bitcast_fusion.4
  103.4 8.8 %collective-permute-done.3 = bf16[384,1024]{1,0:T(8,128)(2,1)} collective-permute-done((bf16[384,1024]{1,0:T(8,128)(2,1)}, bf16[384,1024]{1,0:T(8,128)(2,1)}, u32[]{:S(2)}, u32[]{:S(2)}) %collective-permute-start.3) | collective-permute-done | bytes 786464 | tf_op jit(solution)/shard_map/ppermute | solution.py:22
  113.2 2.0 collective-permute-start.6
  120.0 11.1 %collective-permute-done.5 = bf16[384,1024]{1,0:T(8,128)(2,1)S(1)} collective-permute-done((bf16[384,1024]{1,0:T(8,128)(2,1)}, bf16[384,1024]{1,0:T(8,128)(2,1)S(1)}, u32[]{:S(2)}, u32[]{:S(2)}) %collective-permute-start.5) | collective-permute-done | bytes 786464 | tf_op jit(solution)/shard_map/ppermute | solution.py:22
  131.2 2.1 fusion.61
  133.3 1.9 convolution_convert_fusion.1
  135.2 7.4 %convolution_convert_fusion = bf16[3072,512]{0,1:T(8,128)(2,1)} fusion(bf16[3072,256]{1,0:T(8,128)(2,1)} %get-tuple-element.63, bf16[3072,256]{1,0:T(8,128)(2,1)} %get-tuple-element.64, bf16[3072,512]{0,1:T(8,128)(2,1)S(1)} %convolution_convert_fusion.1, bf16[256,256]{1,0:T(8,128)(2,1)} %get-tuple-element.86, bf16[256,256]{1,0:T(8,128)(2,1)} %get-tuple-element.88, ...), kind=kOutput, calls=%fused_computation.20 | convolution fusion | flops 3236429824 | bytes 10223616 | tf_op jit(solution)/shard_map/dot_general | solution.py:57
  142.8 1.7 copy-done.2
  144.7 3.1 %pad_maximum_fusion = bf16[3072,1024]{0,1:T(8,128)(2,1)} fusion(bf16[3072,256]{0,1:T(8,128)(2,1)S(1)} %get-tuple-element.73, bf16[3072,256]{0,1:T(8,128)(2,1)S(1)} %get-tuple-element.71, bf16[3072,256]{0,1:T(8,128)(2,1)S(1)} %get-tuple-element.72, bf16[3072,256]{0,1:T(8,128)(2,1)S(1)} %get-tuple-element.70), kind=kLoop, calls=%fused_computation.17 | loop fusion | flops 25165824 | bytes 12582912 | tf_op jit(solution)/shard_map/concatenate | solution.py:42
  147.8 8.6 %copy.12 = bf16[3072,1024]{1,0:T(8,128)(2,1)} copy(bf16[3072,1024]{0,1:T(8,128)(2,1)} %pad_maximum_fusion) | data formatting | bytes 12582912 | tf_op jit(solution)/shard_map/concatenate | solution.py:42
  156.5 2.1 fusion.62
  160.7 3.2 %pad_maximum_fusion.1 = bf16[24,128,1024]{2,1,0:T(8,128)(2,1)} fusion(bf16[24,64,1024]{2,1,0:T(8,128)(2,1)S(1)} %bitcast.99, bf16[24,64,512]{2,1,0:T(8,128)(2,1)S(1)} %maximum_negate_fusion, bf16[24,64,512]{2,1,0:T(8,128)(2,1)S(1)} %bitcast.103), kind=kLoop, calls=%fused_computation.18 | loop fusion | flops 18874368 | bytes 12582912 | tf_op jit(solution)/shard_map/concatenate | solution.py:83
  163.9 45.5 %while.10 = (s32[]{:T(128)}, bf16[4,64,24,128]{3,2,1,0:T(8,128)(2,1)}, bf16[4,64,24,128]{3,2,1,0:T(8,128)(2,1)}, s32[4,24]{1,0:T(4,128)}, bf16[48,64,1024]{2,1,0...) while((s32[]{:T(128)}, bf16[4,64,24,128]{3,2,1,0:T(8,128)(2,1)}, ...), condition=%wide.region_4.5_spmd, body=%wide.region_3.4_spmd.sunk | while | flops 403244096 | bytes 18093012 | solution.py:125
  164.6 3.5 %gather_fusion = bf16[24,64,1024]{2,1,0:T(8,128)(2,1)S(1)} fusion(bf16[48,64,1024]{2,1,0:T(8,128)(2,1)} %get-tuple-element.145, s32[1024]{0:T(1024)S(1)} %pad_clamp_fusion.4), kind=kCustom, calls=%fused_computation.clone.1 | custom fusion | bytes 6291552 | tf_op jit(solution)/shard_map/while/body/eval_jaxpr/gather | solution.py:121
  169.2 5.1 %fusion.76 = bf16[1,64,24,128]{3,1,2,0:T(8,128)(2,1)S(1)} fusion(bf16[24,64,1024]{2,1,0:T(8,128)(2,1)S(1)} %gather_fusion, bf16[24,128,1024]{2,1,0:T(8,128)(2,1)} %get-tuple-element.146, bf16[1,64,24,128]{3,2,1,0:T(8,128)(2,1)S(1)} %constant_dynamic-slice_fusion.4), kind=kOutput, calls=%fused_computation.8.clone.1 | convolution fusion | flops 403243008 | bytes 10223616 | tf_op jit(solution)/shard_map/while/body/eval_jaxpr/jbp,jqp->bjq/dot_general | solution.py:122
  176.0 3.5 %gather_fusion = bf16[24,64,1024]{2,1,0:T(8,128)(2,1)S(1)} fusion(bf16[48,64,1024]{2,1,0:T(8,128)(2,1)} %get-tuple-element.145, s32[1024]{0:T(1024)S(1)} %pad_clamp_fusion.4), kind=kCustom, calls=%fused_computation.clone.1 | custom fusion | bytes 6291552 | tf_op jit(solution)/shard_map/while/body/eval_jaxpr/gather | solution.py:121
  180.6 5.1 %fusion.76 = bf16[1,64,24,128]{3,1,2,0:T(8,128)(2,1)S(1)} fusion(bf16[24,64,1024]{2,1,0:T(8,128)(2,1)S(1)} %gather_fusion, bf16[24,128,1024]{2,1,0:T(8,128)(2,1)} %get-tuple-element.146, bf16[1,64,24,128]{3,2,1,0:T(8,128)(2,1)S(1)} %constant_dynamic-slice_fusion.4), kind=kOutput, calls=%fused_computation.8.clone.1 | convolution fusion | flops 403243008 | bytes 10223616 | tf_op jit(solution)/shard_map/while/body/eval_jaxpr/jbp,jqp->bjq/dot_general | solution.py:122
  187.4 3.5 %gather_fusion = bf16[24,64,1024]{2,1,0:T(8,128)(2,1)S(1)} fusion(bf16[48,64,1024]{2,1,0:T(8,128)(2,1)} %get-tuple-element.145, s32[1024]{0:T(1024)S(1)} %pad_clamp_fusion.4), kind=kCustom, calls=%fused_computation.clone.1 | custom fusion | bytes 6291552 | tf_op jit(solution)/shard_map/while/body/eval_jaxpr/gather | solution.py:121
  191.9 5.1 %fusion.76 = bf16[1,64,24,128]{3,1,2,0:T(8,128)(2,1)S(1)} fusion(bf16[24,64,1024]{2,1,0:T(8,128)(2,1)S(1)} %gather_fusion, bf16[24,128,1024]{2,1,0:T(8,128)(2,1)} %get-tuple-element.146, bf16[1,64,24,128]{3,2,1,0:T(8,128)(2,1)S(1)} %constant_dynamic-slice_fusion.4), kind=kOutput, calls=%fused_computation.8.clone.1 | convolution fusion | flops 403243008 | bytes 10223616 | tf_op jit(solution)/shard_map/while/body/eval_jaxpr/jbp,jqp->bjq/dot_general | solution.py:122
  198.7 3.5 %gather_fusion = bf16[24,64,1024]{2,1,0:T(8,128)(2,1)S(1)} fusion(bf16[48,64,1024]{2,1,0:T(8,128)(2,1)} %get-tuple-element.145, s32[1024]{0:T(1024)S(1)} %pad_clamp_fusion.4), kind=kCustom, calls=%fused_computation.clone.1 | custom fusion | bytes 6291552 | tf_op jit(solution)/shard_map/while/body/eval_jaxpr/gather | solution.py:121
  203.3 5.1 %fusion.76 = bf16[1,64,24,128]{3,1,2,0:T(8,128)(2,1)S(1)} fusion(bf16[24,64,1024]{2,1,0:T(8,128)(2,1)S(1)} %gather_fusion, bf16[24,128,1024]{2,1,0:T(8,128)(2,1)} %get-tuple-element.146, bf16[1,64,24,128]{3,2,1,0:T(8,128)(2,1)S(1)} %constant_dynamic-slice_fusion.4), kind=kOutput, calls=%fused_computation.8.clone.1 | convolution fusion | flops 403243008 | bytes 10223616 | tf_op jit(solution)/shard_map/while/body/eval_jaxpr/jbp,jqp->bjq/dot_general | solution.py:122
  209.4 3.0 %copy.25 = bf16[32,8,24,128]{3,1,2,0:T(8,128)(2,1)} copy(bf16[32,8,24,128]{3,2,1,0:T(8,128)(2,1)} %bitcast.33) | data formatting | bytes 3145728
  (87 shorter events, 29.7 us)
Async XLA Ops:
  6.5 1.5 copy-start
  6.5 34.2 %copy-start.4 = (bf16[512,1024]{1,0:T(8,128)(2,1)S(1)}, bf16[512,1024]{1,0:T(8,128)(2,1)}, u32[]{:S(2)}) copy-start(bf16[512,1024]{1,0:T(8,128)(2,1)} %param.14) | copy-start | bytes 3145732
  9.7 28.7 %all-to-all-start = ((bf16[8,64,1024]{2,1,0:T(8,128)(2,1)}), bf16[8,64,1024]{2,1,0:T(8,128)(2,1)S(1)}, u32[]{:S(2)}, u32[]{:S(2)}) async-start(bf16[8,64,1024]{2,1,0:T(8,128)(2,1)} %gather_fusion.1), calls=%async_computation | async-start | bytes 2097152 | tf_op jit(solution)/shard_map/all_to_all | solution.py:106
  39.0 11.6 %collective-permute-start = (bf16[384,1024]{1,0:T(8,128)(2,1)S(1)}, bf16[384,1024]{1,0:T(8,128)(2,1)}, u32[]{:S(2)}, u32[]{:S(2)}) collective-permute-start(bf16[384,1024]{1,0:T(8,128)(2,1)S(1)} %bitcast.104), channel_id=1, source_target_pairs={{0,1},{1,2},{2,3},{3,4},{4,5},{5,6},{6,7},{7,0},{8,9},{9,10},{10,1... | collective-permute-start | bytes 2359304 | tf_op jit(solution)/shard_map/ppermute | solution.py:19
  42.4 51.8 %copy-start.3 = (bf16[256,3072]{1,0:T(8,128)(2,1)S(1)}, bf16[256,3072]{1,0:T(8,128)(2,1)}, u32[]{:S(2)}) copy-start(bf16[256,3072]{1,0:T(8,128)(2,1)} %param.11) | copy-start | bytes 4718596
  42.4 59.5 %all-to-all-start.1 = ((bf16[8,64,1024]{2,1,0:T(8,128)(2,1)}), bf16[8,64,1024]{2,1,0:T(8,128)(2,1)S(1)}, u32[]{:S(2)}, u32[]{:S(2)}) async-start(bf16[8,64,1024]{2,1,0:T(8,128)(2,1)} %gather_fusion.3), calls=%async_computation.1 | async-start | bytes 2097152 | tf_op jit(solution)/shard_map/all_to_all | solution.py:107
  49.1 107.3 %all-gather.2.cloned.1.call-start = ((), (), s32[]{:S(2)}) async-start(), calls=%async_computation.2 | async-start | bytes 3932160 | tf_op jit(solution)/shard_map/all_gather | solution.py:113
  49.1 44.3 %collective-permute-start.1 = (bf16[384,1024]{1,0:T(8,128)(2,1)S(1)}, bf16[384,1024]{1,0:T(8,128)(2,1)}, u32[]{:S(2)}, u32[]{:S(2)}) collective-permute-start(bf16[384,1024]{1,0:T(8,128)(2,1)S(1)} %bitcast.105), channel_id=1, source_target_pairs={{0,7},{1,0},{2,1},{3,2},{4,3},{5,4},{6,5},{7,6},{8,15},{9,8},{10,9... | collective-permute-start | bytes 2359304 | tf_op jit(solution)/shard_map/ppermute | solution.py:22
  50.5 42.9 %copy-start.8 = (bf16[256,256]{1,0:T(8,128)(2,1)}, bf16[256,256]{1,0:T(8,128)(2,1)S(1)}, u32[]{:S(2)}) copy-start(bf16[256,256]{1,0:T(8,128)(2,1)S(1)} %get-tuple-element.84) | copy-start | bytes 393220
  50.5 42.9 %copy-start.10 = (bf16[256,256]{1,0:T(8,128)(2,1)}, bf16[256,256]{1,0:T(8,128)(2,1)S(1)}, u32[]{:S(2)}) copy-start(bf16[256,256]{1,0:T(8,128)(2,1)S(1)} %get-tuple-element.85) | copy-start | bytes 393220
  50.5 45.1 %collective-permute-start.2 = (bf16[384,1024]{1,0:T(8,128)(2,1)}, bf16[384,1024]{1,0:T(8,128)(2,1)}, u32[]{:S(2)}, u32[]{:S(2)}) collective-permute-start(bf16[384,1024]{1,0:T(8,128)(2,1)} %collective-permute-done), channel_id=1, source_target_pairs={{0,1},{1,2},{2,3},{3,4},{4,5},{5,6},{6,7},{7,0},{8,9},{9,10},{10,1... | collective-permute-start | bytes 2359304 | tf_op jit(solution)/shard_map/ppermute | solution.py:19
  54.5 39.0 %copy-start.5 = (bf16[256,512]{1,0:T(8,128)(2,1)}, bf16[256,512]{1,0:T(8,128)(2,1)S(1)}, u32[]{:S(2)}) copy-start(bf16[256,512]{1,0:T(8,128)(2,1)S(1)} %convolution_convert_fusion.2) | copy-start | bytes 786436
  93.4 18.8 %collective-permute-start.3 = (bf16[384,1024]{1,0:T(8,128)(2,1)}, bf16[384,1024]{1,0:T(8,128)(2,1)}, u32[]{:S(2)}, u32[]{:S(2)}) collective-permute-start(bf16[384,1024]{1,0:T(8,128)(2,1)} %collective-permute-done.1), channel_id=1, source_target_pairs={{0,7},{1,0},{2,1},{3,2},{4,3},{5,4},{6,5},{7,6},{8,15},{9,8},{10,9... | collective-permute-start | bytes 2359304 | tf_op jit(solution)/shard_map/ppermute | solution.py:22
  95.7 17.5 %collective-permute-start.4 = (bf16[384,1024]{1,0:T(8,128)(2,1)}, bf16[384,1024]{1,0:T(8,128)(2,1)S(1)}, u32[]{:S(2)}, u32[]{:S(2)}) collective-permute-start(bf16[384,1024]{1,0:T(8,128)(2,1)} %collective-permute-done.2), channel_id=1, source_target_pairs={{0,1},{1,2},{2,3},{3,4},{4,5},{5,6},{6,7},{7,0},{8,9},{9,10},{10,1... | collective-permute-start | bytes 2359304 | tf_op jit(solution)/shard_map/ppermute | solution.py:19
  112.3 18.8 %collective-permute-start.5 = (bf16[384,1024]{1,0:T(8,128)(2,1)}, bf16[384,1024]{1,0:T(8,128)(2,1)S(1)}, u32[]{:S(2)}, u32[]{:S(2)}) collective-permute-start(bf16[384,1024]{1,0:T(8,128)(2,1)} %collective-permute-done.3), channel_id=1, source_target_pairs={{0,7},{1,0},{2,1},{3,2},{4,3},{5,4},{6,5},{7,6},{8,15},{9,8},{10,9... | collective-permute-start | bytes 2359304 | tf_op jit(solution)/shard_map/ppermute | solution.py:22
  113.2 18.0 %collective-permute-start.6 = (bf16[384,1024]{1,0:T(8,128)(2,1)S(1)}, bf16[384,1024]{1,0:T(8,128)(2,1)S(1)}, u32[]{:S(2)}, u32[]{:S(2)}) collective-permute-start(bf16[384,1024]{1,0:T(8,128)(2,1)S(1)} %collective-permute-done.4), channel_id=1, source_target_pairs={{0,1},{1,2},{2,3},{3,4},{4,5},{5,6},{6,7},{7,0},{8,9},{9,10},{10,1... | collective-permute-start | bytes 2359304 | tf_op jit(solution)/shard_map/ppermute | solution.py:19
  131.2 2.1 copy-start.9
  131.2 2.1 copy-start.11
  142.6 1.9 copy-start.2
  156.5 2.1 copy-start.6
  156.5 2.1 copy-start.7
  209.4 3.0 %copy-start.1 = (bf16[512,1024]{1,0:T(8,128)(2,1)S(1)}, bf16[512,1024]{1,0:T(8,128)(2,1)}, u32[]{:S(2)}) copy-start(bf16[512,1024]{1,0:T(8,128)(2,1)} %param.13) | copy-start | bytes 3145732
Sparse Core Ops, SparseCore 0:
  103.6 42.5 all-gather.1
